TPU v7x, 256 devices: a whole 4x4x8 slice. The times are simulated.
256 devices in a mesh: ctx: 16 (over z, core), head: 16 (over x, y).
Axes of the slice: x: 4, y: 4, z: 8, core: 2. Of those that a mesh axis runs over, the one named last changes fastest.
Arguments:
- x_in: bfloat16 [32768, 8192], P(('ctx', 'head')), may hold values from -6 to 6
- b_in: bfloat16 [32768, 8, 128], P(('ctx', 'head')), may hold values from -5 to 5
- c_in: bfloat16 [32768, 8, 128], P(('ctx', 'head')), may hold values from -0.5 to 0.5
- dt_raw: bfloat16 [32768, 128], P(('ctx', 'head')), may hold values from -2 to 335
- decay_rate: float32 [128], replicated, may hold values from 0 to 1
- dt_bias: float32 [128], replicated, may hold values from -6 to -2
- skip_gain: float32 [128], replicated, may hold values from 0.5 to 1.5
Outputs:
- y_out: bfloat16 [32768, 8192], P(('ctx', 'head'))
All inputs are finite; a program needn't handle non-finite values.
Results may differ from a plain program's by a relative error of at most 0.012.
Values may be sent and summed in bfloat16 or wider, within the bound.
A program may use at most 128 MiB of HBM per device.

v0:
```python
import jax
import jax.numpy as jnp
from jax import lax
from jax.sharding import PartitionSpec as P

STRETCH = 256


def from_behind(block, axis, distance):
    devices = range(lax.axis_size(axis))
    route = [(i - distance, i) for i in devices if i - distance in devices]
    return lax.ppermute(block, axis, route)


def block_step(state_now, inputs):
    x_block, b_block, c_block, dt_block, cum_block = inputs
    positions = jnp.arange(STRETCH)
    causal = (positions[:, None] >= positions[None, :])[:, :, None]
    scores = jnp.dot(c_block, b_block.T, preferred_element_type=jnp.float32)
    spans = cum_block[:, None, :] - cum_block[None, :, :]
    decays = jnp.where(causal, jnp.exp(jnp.where(causal, spans, 0.0)), 0.0)
    weights = (scores[:, :, None] * decays * dt_block[None, :, :]).astype(jnp.bfloat16)
    y_inside = jnp.einsum("ijh,jhp->ihp", weights, x_block, preferred_element_type=jnp.float32)
    y_state = jnp.exp(cum_block)[:, :, None] * jnp.einsum(
        "in,hpn->ihp", c_block.astype(jnp.float32), state_now, precision=lax.Precision.HIGHEST
    )
    end_weight = jnp.exp(cum_block[-1][None, :] - cum_block) * dt_block
    b_scaled = (b_block.astype(jnp.float32)[:, None, :] * end_weight[:, :, None]).astype(
        jnp.bfloat16
    )
    state_add = jnp.einsum("jhn,jhp->hpn", b_scaled, x_block, preferred_element_type=jnp.float32)
    state_next = jnp.exp(cum_block[-1])[:, None, None] * state_now + state_add
    return (state_next, y_inside + y_state)


def group_scan(inputs):
    x_groups = inputs[0]
    state_start = jnp.zeros((x_groups.shape[2], x_groups.shape[3], inputs[1].shape[2]), jnp.float32)
    final_state, outputs = lax.scan(block_step, state_start, inputs)
    return (outputs, final_state)


def block_scan(x_local, b_local, c_local, dt_local, rate_local, bias_local):
    row_count = x_local.shape[0]
    head_count = dt_local.shape[1]
    groups = b_local.shape[1]
    state_size = b_local.shape[2]
    head_width = x_local.shape[1] // head_count
    per_group = head_count // groups
    blocks = row_count // STRETCH
    step_dt = jax.nn.softplus(dt_local.astype(jnp.float32) + bias_local[None, :])
    log_decay = -rate_local[None, :] * step_dt
    within = jnp.cumsum(log_decay.reshape(blocks, STRETCH, head_count), axis=1)
    totals = within[:, -1, :]
    before = jnp.cumsum(totals, axis=0) - totals
    running = (within + before[:, None, :]).reshape(row_count, head_count)
    x_groups = x_local.reshape(blocks, STRETCH, groups, per_group, head_width).transpose(
        2, 0, 1, 3, 4
    )
    b_groups = b_local.reshape(blocks, STRETCH, groups, state_size).transpose(2, 0, 1, 3)
    c_groups = c_local.reshape(blocks, STRETCH, groups, state_size).transpose(2, 0, 1, 3)
    dt_groups = step_dt.reshape(blocks, STRETCH, groups, per_group).transpose(2, 0, 1, 3)
    cum_groups = within.reshape(blocks, STRETCH, groups, per_group).transpose(2, 0, 1, 3)
    outputs, finals = lax.map(group_scan, (x_groups, b_groups, c_groups, dt_groups, cum_groups))
    partial_value = outputs.transpose(1, 2, 0, 3, 4).reshape(row_count, head_count, head_width)
    return (
        partial_value,
        running,
        finals.reshape(head_count, head_width, state_size),
        jnp.sum(log_decay, axis=0),
    )


def per_device(x_in, b_in, c_in, dt_raw, decay_rate, dt_bias, skip_gain):
    head_shards = lax.axis_size("head")
    head_index = lax.axis_index("head")
    row_count = x_in.shape[0]
    head_total = dt_raw.shape[1]
    group_total = b_in.shape[1]
    state_size = b_in.shape[2]
    head_width = x_in.shape[1] // head_total
    local_heads = head_total // head_shards
    local_groups = max(1, local_heads * group_total // head_total)
    x_split = x_in.reshape(row_count, head_shards, local_heads * head_width)
    dt_split = dt_raw.reshape(row_count, head_shards, local_heads)

    def spread(values):
        values = jnp.repeat(values, head_shards // group_total, axis=1)
        return values.reshape(row_count, head_shards, local_groups, state_size)

    x_local, b_local, c_local, dt_local = (
        lax.all_to_all(x_split, "head", split_axis=1, concat_axis=0, tiled=True),
        lax.all_to_all(spread(b_in), "head", split_axis=1, concat_axis=0, tiled=True),
        lax.all_to_all(spread(c_in), "head", split_axis=1, concat_axis=0, tiled=True),
        lax.all_to_all(dt_split, "head", split_axis=1, concat_axis=0, tiled=True),
    )
    ctx_rows = x_local.shape[0]
    b_local = b_local.reshape(ctx_rows, local_groups, state_size)
    c_local = c_local.reshape(ctx_rows, local_groups, state_size)
    x_local = x_local.reshape(ctx_rows, local_heads * head_width)
    dt_local = dt_local.reshape(ctx_rows, local_heads)
    rate_local = lax.dynamic_slice_in_dim(decay_rate, head_index * local_heads, local_heads)
    bias_local = lax.dynamic_slice_in_dim(dt_bias, head_index * local_heads, local_heads)
    skip_local = lax.dynamic_slice_in_dim(skip_gain, head_index * local_heads, local_heads)
    partial_value, running, shard_state, shard_log = block_scan(
        x_local, b_local, c_local, dt_local, rate_local, bias_local
    )
    shard_decay = jnp.exp(shard_log)[:, None, None]

    def pass_along(index, folded):
        outgoing, incoming = folded
        incoming = from_behind(outgoing.astype(jnp.bfloat16), "ctx", 1).astype(outgoing.dtype)
        return (shard_decay * incoming + shard_state, incoming)

    passed, state_in = lax.fori_loop(
        0, lax.axis_size("ctx") - 1, pass_along, (shard_state, jnp.zeros_like(shard_state))
    )
    per_group = local_heads // local_groups
    grouped_in = state_in.reshape(local_groups, per_group, head_width, state_size)
    carried = jnp.einsum(
        "rgn,ghpn->rghp", c_local.astype(jnp.float32), grouped_in, precision=lax.Precision.HIGHEST
    )
    correction = jnp.exp(running)[:, :, None] * carried.reshape(ctx_rows, local_heads, head_width)
    direct = skip_local[None, :, None] * x_local.reshape(ctx_rows, local_heads, head_width).astype(
        jnp.float32
    )
    y_local = (
        (partial_value + correction + direct)
        .astype(jnp.bfloat16)
        .reshape(ctx_rows, local_heads * head_width)
    )
    return lax.all_to_all(y_local, "head", split_axis=0, concat_axis=1, tiled=True)


def solution(mesh):
    in_specs = (
        P(("ctx", "head"), None),
        P(("ctx", "head"), None, None),
        P(("ctx", "head"), None, None),
        P(("ctx", "head"), None),
        P(),
        P(),
        P(),
    )
    out_specs = P(("ctx", "head"), None)
    return jax.shard_map(
        per_device, mesh=mesh, in_specs=in_specs, out_specs=out_specs, check_vma=False
    )
```

profile of v0, /device:TPU:97, one launch (start us, length us, event | category | flops | bytes accessed | tf_op | source)
XLA Modules:
  0.0 409.0 jit_solution(17417598340440923269)
XLA Ops:
  1.6 6.8 %all-to-all-start = ((bf16[128,16,8]{0,2,1:T(8,128)(2,1)}), bf16[128,16,8]{0,2,1:T(8,128)(2,1)S(1)}, u32[]{:S(2)}, u32[]{:S(2)}) async-start(bf16[128,16,8]{0,2,1:T(8,128)(2,1)} %bitcast.1), calls=%async_computation | async-start | bytes 65536 | tf_op jit(solution)/shard_map/all_to_all | solution.py:95
  9.4 5.5 %all-to-all-done = bf16[128,16,8]{0,2,1:T(8,128)(2,1)S(1)} async-done(((bf16[128,16,8]{0,2,1:T(8,128)(2,1)}), bf16[128,16,8]{0,2,1:T(8,128)(2,1)S(1)}, u32[]{:S(2)}, u32[]{:S(2)}) %all-to-all-start) | async-done | bytes 32800 | tf_op jit(solution)/shard_map/all_to_all | solution.py:95
  15.8 4.3 %all-to-all-start.2 = ((bf16[128,16,1,128]{3,0,2,1:T(8,128)(2,1)}), bf16[128,16,1,128]{3,0,2,1:T(8,128)(2,1)}, u32[]{:S(2)}, u32[]{:S(2)}) async-start(bf16[128,16,1,128]{3,0,2,1:T(8,128)(2,1)} %bitcast.13), calls=%async_computation.2 | async-start | bytes 1048576 | tf_op jit(solution)/shard_map/all_to_all | solution.py:93
  20.0 2.4 copy.51
  22.5 6.7 %all-to-all-done.2 = bf16[128,16,1,128]{3,0,2,1:T(8,128)(2,1)} async-done(((bf16[128,16,1,128]{3,0,2,1:T(8,128)(2,1)}), bf16[128,16,1,128]{3,0,2,1:T(8,128)(2,1)}, u32[]{:S(2)}, u32[]{:S(2)}) %all-to-all-start.2) | async-done | bytes 524320 | tf_op jit(solution)/shard_map/all_to_all | solution.py:93
  29.2 3.9 all-to-all-start.1
  34.3 4.5 %reduce-window.6 = f32[8,8,2,128]{3,1,2,0:T(8,128)S(1)} reduce-window(f32[8,8,2,128]{3,1,2,0:T(8,128)S(1)} %get-tuple-element.200, f32[]{:T(128)} %constant.49.clone.1), window={size=1x1x1x128 pad=0_0x0_0x0_0x127_0}, to_apply=%region_0.1 | reduce-window | flops 2080768 | bytes 131076 | tf_op jit(solution)/shard_map/reduce-window
  39.4 18.9 %all-to-all-done.1 = bf16[128,16,512]{0,2,1:T(8,128)(2,1)S(1)} async-done(((bf16[128,16,512]{0,2,1:T(8,128)(2,1)}), bf16[128,16,512]{0,2,1:T(8,128)(2,1)S(1)}, u32[]{:S(2)}, u32[]{:S(2)}) %all-to-all-start.1) | async-done | bytes 2097184 | tf_op jit(solution)/shard_map/all_to_all | solution.py:92
  59.2 6.8 %all-to-all-start.3 = ((bf16[128,16,1,128]{3,0,2,1:T(8,128)(2,1)}), bf16[128,16,1,128]{3,0,2,1:T(8,128)(2,1)S(1)}, u32[]{:S(2)}, u32[]{:S(2)}) async-start(bf16[128,16,1,128]{3,0,2,1:T(8,128)(2,1)} %bitcast.17), calls=%async_computation.3 | async-start | bytes 1048576 | tf_op jit(solution)/shard_map/all_to_all | solution.py:94
  66.6 2.9 copy.67
  70.2 2.7 copy.52
  72.9 4.1 squeeze.44
  76.9 3.4 copy.55
  80.3 153.2 %while.35 = (s32[]{:T(128)}, f32[8,64,128]{2,1,0:T(8,128)S(1)}, f32[8,256,8,64]{1,0,3,2:T(8,128)}, f32[8,256,8]{1,2,0:T(8,128)S(1)}, bf16[8,256,8,64]{1,3,2,0:T(...) while((s32[]{:T(128)}, f32[8,64,128]{2,1,0:T(8,128)S(1)}, ...), condition=%wide.region_3.4_spmd.clone, body=%wide.region_2.3_spmd.clone.sunk | while | flops 323063808 | bytes 6260080 | solution.py:39
  84.4 1.8 fusion.63
  86.7 12.7 %dynamic_update_slice.12 = f32[8,256,8,64]{1,0,3,2:T(8,128)} dynamic-update-slice(f32[8,256,8,64]{1,0,3,2:T(8,128)} %get-tuple-element.305, f32[1,256,8,64]{1,0,3,2:T(1,128)S(1)} %copy.77, s32[]{:T(128)S(6)} %copy.82, s32[]{:T(128)} %constant.47.clone.1..sunk, s32[]{:T(128)} %constant.47.clone.1..sunk, s32[]{:T(128)} %constant.47.clone.1..sunk) | dynamic-update-slice | bytes 1048580 | tf_op jit(solution)/shard_map/while/body/eval_jaxpr/while/body/jit(dynamic_update_index_in_dim)/dynamic_update_slice | solution.py:39
  103.6 1.8 fusion.63
  105.9 12.7 %dynamic_update_slice.12 = f32[8,256,8,64]{1,0,3,2:T(8,128)} dynamic-update-slice(f32[8,256,8,64]{1,0,3,2:T(8,128)} %get-tuple-element.305, f32[1,256,8,64]{1,0,3,2:T(1,128)S(1)} %copy.77, s32[]{:T(128)S(6)} %copy.82, s32[]{:T(128)} %constant.47.clone.1..sunk, s32[]{:T(128)} %constant.47.clone.1..sunk, s32[]{:T(128)} %constant.47.clone.1..sunk) | dynamic-update-slice | bytes 1048580 | tf_op jit(solution)/shard_map/while/body/eval_jaxpr/while/body/jit(dynamic_update_index_in_dim)/dynamic_update_slice | solution.py:39
  122.7 1.8 fusion.63
  125.1 12.7 %dynamic_update_slice.12 = f32[8,256,8,64]{1,0,3,2:T(8,128)} dynamic-update-slice(f32[8,256,8,64]{1,0,3,2:T(8,128)} %get-tuple-element.305, f32[1,256,8,64]{1,0,3,2:T(1,128)S(1)} %copy.77, s32[]{:T(128)S(6)} %copy.82, s32[]{:T(128)} %constant.47.clone.1..sunk, s32[]{:T(128)} %constant.47.clone.1..sunk, s32[]{:T(128)} %constant.47.clone.1..sunk) | dynamic-update-slice | bytes 1048580 | tf_op jit(solution)/shard_map/while/body/eval_jaxpr/while/body/jit(dynamic_update_index_in_dim)/dynamic_update_slice | solution.py:39
  144.2 12.7 %dynamic_update_slice.12 = f32[8,256,8,64]{1,0,3,2:T(8,128)} dynamic-update-slice(f32[8,256,8,64]{1,0,3,2:T(8,128)} %get-tuple-element.305, f32[1,256,8,64]{1,0,3,2:T(1,128)S(1)} %copy.77, s32[]{:T(128)S(6)} %copy.82, s32[]{:T(128)} %constant.47.clone.1..sunk, s32[]{:T(128)} %constant.47.clone.1..sunk, s32[]{:T(128)} %constant.47.clone.1..sunk) | dynamic-update-slice | bytes 1048580 | tf_op jit(solution)/shard_map/while/body/eval_jaxpr/while/body/jit(dynamic_update_index_in_dim)/dynamic_update_slice | solution.py:39
  161.1 1.8 fusion.63
  163.4 12.7 %dynamic_update_slice.12 = f32[8,256,8,64]{1,0,3,2:T(8,128)} dynamic-update-slice(f32[8,256,8,64]{1,0,3,2:T(8,128)} %get-tuple-element.305, f32[1,256,8,64]{1,0,3,2:T(1,128)S(1)} %copy.77, s32[]{:T(128)S(6)} %copy.82, s32[]{:T(128)} %constant.47.clone.1..sunk, s32[]{:T(128)} %constant.47.clone.1..sunk, s32[]{:T(128)} %constant.47.clone.1..sunk) | dynamic-update-slice | bytes 1048580 | tf_op jit(solution)/shard_map/while/body/eval_jaxpr/while/body/jit(dynamic_update_index_in_dim)/dynamic_update_slice | solution.py:39
  180.2 1.8 fusion.63
  182.5 12.7 %dynamic_update_slice.12 = f32[8,256,8,64]{1,0,3,2:T(8,128)} dynamic-update-slice(f32[8,256,8,64]{1,0,3,2:T(8,128)} %get-tuple-element.305, f32[1,256,8,64]{1,0,3,2:T(1,128)S(1)} %copy.77, s32[]{:T(128)S(6)} %copy.82, s32[]{:T(128)} %constant.47.clone.1..sunk, s32[]{:T(128)} %constant.47.clone.1..sunk, s32[]{:T(128)} %constant.47.clone.1..sunk) | dynamic-update-slice | bytes 1048580 | tf_op jit(solution)/shard_map/while/body/eval_jaxpr/while/body/jit(dynamic_update_index_in_dim)/dynamic_update_slice | solution.py:39
  201.7 12.7 %dynamic_update_slice.12 = f32[8,256,8,64]{1,0,3,2:T(8,128)} dynamic-update-slice(f32[8,256,8,64]{1,0,3,2:T(8,128)} %get-tuple-element.305, f32[1,256,8,64]{1,0,3,2:T(1,128)S(1)} %copy.77, s32[]{:T(128)S(6)} %copy.82, s32[]{:T(128)} %constant.47.clone.1..sunk, s32[]{:T(128)} %constant.47.clone.1..sunk, s32[]{:T(128)} %constant.47.clone.1..sunk) | dynamic-update-slice | bytes 1048580 | tf_op jit(solution)/shard_map/while/body/eval_jaxpr/while/body/jit(dynamic_update_index_in_dim)/dynamic_update_slice | solution.py:39
  218.5 1.8 fusion.63
  220.8 12.7 %dynamic_update_slice.12 = f32[8,256,8,64]{1,0,3,2:T(8,128)} dynamic-update-slice(f32[8,256,8,64]{1,0,3,2:T(8,128)} %get-tuple-element.305, f32[1,256,8,64]{1,0,3,2:T(1,128)S(1)} %copy.77, s32[]{:T(128)S(6)} %copy.82, s32[]{:T(128)} %constant.47.clone.1..sunk, s32[]{:T(128)} %constant.47.clone.1..sunk, s32[]{:T(128)} %constant.47.clone.1..sunk) | dynamic-update-slice | bytes 1048580 | tf_op jit(solution)/shard_map/while/body/eval_jaxpr/while/body/jit(dynamic_update_index_in_dim)/dynamic_update_slice | solution.py:39
  233.6 4.8 %reshape_transpose.3 = f32[16,128,512]{1,0,2:T(8,128)} reshape(f32[8,256,8,64]{1,0,3,2:T(8,128)} %get-tuple-element.98) | data formatting | bytes 8388608 | tf_op jit(solution)/shard_map/reshape;transpose | solution.py:65
  238.4 125.6 %while.34 = (s32[]{:T(128)}, bf16[8,64,128]{2,1,0:T(8,128)(2,1)S(1)}, f32[8,64,128]{2,1,0:T(8,128)}, f32[8,1,1]{0,2,1:T(1,128)S(1)}, f32[8,64,128]{2,1,0:T(8,128)S(1)}, /*index=5*/s32[]{:T(128)}) while((s32[]{:T(128)}, bf16[8,64,128]{2,1,0:T(8,128)(2,1)S(1)}, f32[8,64,128]{2,1,0:T(8,128)}, f32[8,1,1]{0,2,1:T(1,128)S(1)}, ...), condition=%wide.region_7.8_spmd, body=%wide.region_6.7_spmd.sunk | while | flops 262146 | bytes 1310861 | solution.py:115
  238.4 7.9 %collective-permute-start = (bf16[8,64,128]{2,1,0:T(8,128)(2,1)S(1)}, bf16[8,64,128]{2,1,0:T(8,128)(2,1)S(1)}, u32[]{:S(2)}, u32[]{:S(2)}) collective-permute-start(bf16[8,64,128]{2,1,0:T(8,128)(2,1)S(1)} %get-tuple-element.332), channel_id=1, source_target_pairs={{0,16},{16,32},{32,48},{48,64},{64,80},{80,96},{96,112},{112,128},... | collective-permute-start | bytes 393224 | tf_op jit(solution)/shard_map/while/body/eval_jaxpr/ppermute | solution.py:12
  246.3 1.9 collective-permute-done
  249.0 5.6 %collective-permute-start = (bf16[8,64,128]{2,1,0:T(8,128)(2,1)S(1)}, bf16[8,64,128]{2,1,0:T(8,128)(2,1)S(1)}, u32[]{:S(2)}, u32[]{:S(2)}) collective-permute-start(bf16[8,64,128]{2,1,0:T(8,128)(2,1)S(1)} %get-tuple-element.332), channel_id=1, source_target_pairs={{0,16},{16,32},{32,48},{48,64},{64,80},{80,96},{96,112},{112,128},... | collective-permute-start | bytes 393224 | tf_op jit(solution)/shard_map/while/body/eval_jaxpr/ppermute | solution.py:12
  254.5 1.9 collective-permute-done
  257.2 5.6 %collective-permute-start = (bf16[8,64,128]{2,1,0:T(8,128)(2,1)S(1)}, bf16[8,64,128]{2,1,0:T(8,128)(2,1)S(1)}, u32[]{:S(2)}, u32[]{:S(2)}) collective-permute-start(bf16[8,64,128]{2,1,0:T(8,128)(2,1)S(1)} %get-tuple-element.332), channel_id=1, source_target_pairs={{0,16},{16,32},{32,48},{48,64},{64,80},{80,96},{96,112},{112,128},... | collective-permute-start | bytes 393224 | tf_op jit(solution)/shard_map/while/body/eval_jaxpr/ppermute | solution.py:12
  262.8 1.9 collective-permute-done
  265.4 5.6 %collective-permute-start = (bf16[8,64,128]{2,1,0:T(8,128)(2,1)S(1)}, bf16[8,64,128]{2,1,0:T(8,128)(2,1)S(1)}, u32[]{:S(2)}, u32[]{:S(2)}) collective-permute-start(bf16[8,64,128]{2,1,0:T(8,128)(2,1)S(1)} %get-tuple-element.332), channel_id=1, source_target_pairs={{0,16},{16,32},{32,48},{48,64},{64,80},{80,96},{96,112},{112,128},... | collective-permute-start | bytes 393224 | tf_op jit(solution)/shard_map/while/body/eval_jaxpr/ppermute | solution.py:12
  271.0 1.9 collective-permute-done
  273.6 5.6 %collective-permute-start = (bf16[8,64,128]{2,1,0:T(8,128)(2,1)S(1)}, bf16[8,64,128]{2,1,0:T(8,128)(2,1)S(1)}, u32[]{:S(2)}, u32[]{:S(2)}) collective-permute-start(bf16[8,64,128]{2,1,0:T(8,128)(2,1)S(1)} %get-tuple-element.332), channel_id=1, source_target_pairs={{0,16},{16,32},{32,48},{48,64},{64,80},{80,96},{96,112},{112,128},... | collective-permute-start | bytes 393224 | tf_op jit(solution)/shard_map/while/body/eval_jaxpr/ppermute | solution.py:12
  279.2 1.9 collective-permute-done
  281.8 5.6 %collective-permute-start = (bf16[8,64,128]{2,1,0:T(8,128)(2,1)S(1)}, bf16[8,64,128]{2,1,0:T(8,128)(2,1)S(1)}, u32[]{:S(2)}, u32[]{:S(2)}) collective-permute-start(bf16[8,64,128]{2,1,0:T(8,128)(2,1)S(1)} %get-tuple-element.332), channel_id=1, source_target_pairs={{0,16},{16,32},{32,48},{48,64},{64,80},{80,96},{96,112},{112,128},... | collective-permute-start | bytes 393224 | tf_op jit(solution)/shard_map/while/body/eval_jaxpr/ppermute | solution.py:12
  287.4 1.9 collective-permute-done
  290.1 5.6 %collective-permute-start = (bf16[8,64,128]{2,1,0:T(8,128)(2,1)S(1)}, bf16[8,64,128]{2,1,0:T(8,128)(2,1)S(1)}, u32[]{:S(2)}, u32[]{:S(2)}) collective-permute-start(bf16[8,64,128]{2,1,0:T(8,128)(2,1)S(1)} %get-tuple-element.332), channel_id=1, source_target_pairs={{0,16},{16,32},{32,48},{48,64},{64,80},{80,96},{96,112},{112,128},... | collective-permute-start | bytes 393224 | tf_op jit(solution)/shard_map/while/body/eval_jaxpr/ppermute | solution.py:12
  295.6 1.9 collective-permute-done
  298.3 5.6 %collective-permute-start = (bf16[8,64,128]{2,1,0:T(8,128)(2,1)S(1)}, bf16[8,64,128]{2,1,0:T(8,128)(2,1)S(1)}, u32[]{:S(2)}, u32[]{:S(2)}) collective-permute-start(bf16[8,64,128]{2,1,0:T(8,128)(2,1)S(1)} %get-tuple-element.332), channel_id=1, source_target_pairs={{0,16},{16,32},{32,48},{48,64},{64,80},{80,96},{96,112},{112,128},... | collective-permute-start | bytes 393224 | tf_op jit(solution)/shard_map/while/body/eval_jaxpr/ppermute | solution.py:12
  303.8 1.9 collective-permute-done
  306.5 5.6 %collective-permute-start = (bf16[8,64,128]{2,1,0:T(8,128)(2,1)S(1)}, bf16[8,64,128]{2,1,0:T(8,128)(2,1)S(1)}, u32[]{:S(2)}, u32[]{:S(2)}) collective-permute-start(bf16[8,64,128]{2,1,0:T(8,128)(2,1)S(1)} %get-tuple-element.332), channel_id=1, source_target_pairs={{0,16},{16,32},{32,48},{48,64},{64,80},{80,96},{96,112},{112,128},... | collective-permute-start | bytes 393224 | tf_op jit(solution)/shard_map/while/body/eval_jaxpr/ppermute | solution.py:12
  312.0 1.9 collective-permute-done
  314.7 5.6 %collective-permute-start = (bf16[8,64,128]{2,1,0:T(8,128)(2,1)S(1)}, bf16[8,64,128]{2,1,0:T(8,128)(2,1)S(1)}, u32[]{:S(2)}, u32[]{:S(2)}) collective-permute-start(bf16[8,64,128]{2,1,0:T(8,128)(2,1)S(1)} %get-tuple-element.332), channel_id=1, source_target_pairs={{0,16},{16,32},{32,48},{48,64},{64,80},{80,96},{96,112},{112,128},... | collective-permute-start | bytes 393224 | tf_op jit(solution)/shard_map/while/body/eval_jaxpr/ppermute | solution.py:12
  320.3 1.9 collective-permute-done
  322.9 5.6 %collective-permute-start = (bf16[8,64,128]{2,1,0:T(8,128)(2,1)S(1)}, bf16[8,64,128]{2,1,0:T(8,128)(2,1)S(1)}, u32[]{:S(2)}, u32[]{:S(2)}) collective-permute-start(bf16[8,64,128]{2,1,0:T(8,128)(2,1)S(1)} %get-tuple-element.332), channel_id=1, source_target_pairs={{0,16},{16,32},{32,48},{48,64},{64,80},{80,96},{96,112},{112,128},... | collective-permute-start | bytes 393224 | tf_op jit(solution)/shard_map/while/body/eval_jaxpr/ppermute | solution.py:12
  328.5 1.9 collective-permute-done
  331.1 5.6 %collective-permute-start = (bf16[8,64,128]{2,1,0:T(8,128)(2,1)S(1)}, bf16[8,64,128]{2,1,0:T(8,128)(2,1)S(1)}, u32[]{:S(2)}, u32[]{:S(2)}) collective-permute-start(bf16[8,64,128]{2,1,0:T(8,128)(2,1)S(1)} %get-tuple-element.332), channel_id=1, source_target_pairs={{0,16},{16,32},{32,48},{48,64},{64,80},{80,96},{96,112},{112,128},... | collective-permute-start | bytes 393224 | tf_op jit(solution)/shard_map/while/body/eval_jaxpr/ppermute | solution.py:12
  336.7 1.9 collective-permute-done
  339.4 5.6 %collective-permute-start = (bf16[8,64,128]{2,1,0:T(8,128)(2,1)S(1)}, bf16[8,64,128]{2,1,0:T(8,128)(2,1)S(1)}, u32[]{:S(2)}, u32[]{:S(2)}) collective-permute-start(bf16[8,64,128]{2,1,0:T(8,128)(2,1)S(1)} %get-tuple-element.332), channel_id=1, source_target_pairs={{0,16},{16,32},{32,48},{48,64},{64,80},{80,96},{96,112},{112,128},... | collective-permute-start | bytes 393224 | tf_op jit(solution)/shard_map/while/body/eval_jaxpr/ppermute | solution.py:12
  344.9 1.9 collective-permute-done
  347.6 5.6 %collective-permute-start = (bf16[8,64,128]{2,1,0:T(8,128)(2,1)S(1)}, bf16[8,64,128]{2,1,0:T(8,128)(2,1)S(1)}, u32[]{:S(2)}, u32[]{:S(2)}) collective-permute-start(bf16[8,64,128]{2,1,0:T(8,128)(2,1)S(1)} %get-tuple-element.332), channel_id=1, source_target_pairs={{0,16},{16,32},{32,48},{48,64},{64,80},{80,96},{96,112},{112,128},... | collective-permute-start | bytes 393224 | tf_op jit(solution)/shard_map/while/body/eval_jaxpr/ppermute | solution.py:12
  353.1 1.9 collective-permute-done
  355.8 5.6 %collective-permute-start = (bf16[8,64,128]{2,1,0:T(8,128)(2,1)S(1)}, bf16[8,64,128]{2,1,0:T(8,128)(2,1)S(1)}, u32[]{:S(2)}, u32[]{:S(2)}) collective-permute-start(bf16[8,64,128]{2,1,0:T(8,128)(2,1)S(1)} %get-tuple-element.332), channel_id=1, source_target_pairs={{0,16},{16,32},{32,48},{48,64},{64,80},{80,96},{96,112},{112,128},... | collective-permute-start | bytes 393224 | tf_op jit(solution)/shard_map/while/body/eval_jaxpr/ppermute | solution.py:12
  361.3 1.9 collective-permute-done
  364.0 2.7 fusion.43
  370.2 3.9 fusion.31
  374.1 32.0 %all_to_all.70 = bf16[16,128,512]{1,2,0:T(8,128)(2,1)S(1)} all-to-all(bf16[16,128,512]{1,2,0:T(8,128)(2,1)S(1)} %fusion.31), channel_id=1, replica_groups=mesh['ctx'=16,'head'=16] {'head'}, dimensions={0} | all-to-all | bytes 4194304 | tf_op jit(solution)/shard_map/all_to_all | solution.py:132
  406.1 2.9 copy.60
  (148 shorter events, 62.2 us)
Async XLA Ops:
  0.0 20.0 %copy-start.2 = (bf16[128,8192]{1,0:T(8,128)(2,1)S(1)}, bf16[128,8192]{1,0:T(8,128)(2,1)}, u32[]{:S(2)}) copy-start(bf16[128,8192]{1,0:T(8,128)(2,1)} %param.11) | copy-start | bytes 6291460
  1.6 13.2 %all-to-all-start = ((bf16[128,16,8]{0,2,1:T(8,128)(2,1)}), bf16[128,16,8]{0,2,1:T(8,128)(2,1)S(1)}, u32[]{:S(2)}, u32[]{:S(2)}) async-start(bf16[128,16,8]{0,2,1:T(8,128)(2,1)} %bitcast.1), calls=%async_computation | async-start | bytes 65536 | tf_op jit(solution)/shard_map/all_to_all | solution.py:95
  14.9 19.3 %copy-start.4 = (bf16[128,16,8]{0,2,1:T(8,128)(2,1)}, bf16[128,16,8]{0,2,1:T(8,128)(2,1)S(1)}, u32[]{:S(2)}) copy-start(bf16[128,16,8]{0,2,1:T(8,128)(2,1)S(1)} %all-to-all-done) | copy-start | bytes 98308
  15.8 13.5 %all-to-all-start.2 = ((bf16[128,16,1,128]{3,0,2,1:T(8,128)(2,1)}), bf16[128,16,1,128]{3,0,2,1:T(8,128)(2,1)}, u32[]{:S(2)}, u32[]{:S(2)}) async-start(bf16[128,16,1,128]{3,0,2,1:T(8,128)(2,1)} %bitcast.13), calls=%async_computation.2 | async-start | bytes 1048576 | tf_op jit(solution)/shard_map/all_to_all | solution.py:93
  29.2 3.9 copy-start.3
  29.2 4.0 copy-start.8
  29.2 4.1 copy-start.9
  29.2 4.9 %copy-start.10 = (f32[128]{0:T(128)S(1)}, f32[128]{0:T(128)}, u32[]{:S(2)}) copy-start(f32[128]{0:T(128)} %param.15) | copy-start | bytes 1540
  29.2 29.0 %all-to-all-start.1 = ((bf16[128,16,512]{0,2,1:T(8,128)(2,1)}), bf16[128,16,512]{0,2,1:T(8,128)(2,1)S(1)}, u32[]{:S(2)}, u32[]{:S(2)}) async-start(bf16[128,16,512]{0,2,1:T(8,128)(2,1)} %bitcast.143), calls=%async_computation.1 | async-start | bytes 4194304 | tf_op jit(solution)/shard_map/all_to_all | solution.py:92
  59.2 21.1 %all-to-all-start.3 = ((bf16[128,16,1,128]{3,0,2,1:T(8,128)(2,1)}), bf16[128,16,1,128]{3,0,2,1:T(8,128)(2,1)S(1)}, u32[]{:S(2)}, u32[]{:S(2)}) async-start(bf16[128,16,1,128]{3,0,2,1:T(8,128)(2,1)} %bitcast.17), calls=%async_computation.3 | async-start | bytes 1048576 | tf_op jit(solution)/shard_map/all_to_all | solution.py:94
  66.5 2.9 copy-start.5
  233.6 4.8 %copy-start.6 = (f32[8,1,1]{0,2,1:T(1,128)S(1)}, f32[8,1,1]{0,2,1:T(1,128)}, u32[]{:S(2)}) copy-start(f32[8,1,1]{0,2,1:T(1,128)} %exponential_bitcast_fusion) | copy-start | bytes 100
  238.4 9.9 %collective-permute-start = (bf16[8,64,128]{2,1,0:T(8,128)(2,1)S(1)}, bf16[8,64,128]{2,1,0:T(8,128)(2,1)S(1)}, u32[]{:S(2)}, u32[]{:S(2)}) collective-permute-start(bf16[8,64,128]{2,1,0:T(8,128)(2,1)S(1)} %get-tuple-element.332), channel_id=1, source_target_pairs={{0,16},{16,32},{32,48},{48,64},{64,80},{80,96},{96,112},{112,128},... | collective-permute-start | bytes 393224 | tf_op jit(solution)/shard_map/while/body/eval_jaxpr/ppermute | solution.py:12
  249.0 7.5 %collective-permute-start = (bf16[8,64,128]{2,1,0:T(8,128)(2,1)S(1)}, bf16[8,64,128]{2,1,0:T(8,128)(2,1)S(1)}, u32[]{:S(2)}, u32[]{:S(2)}) collective-permute-start(bf16[8,64,128]{2,1,0:T(8,128)(2,1)S(1)} %get-tuple-element.332), channel_id=1, source_target_pairs={{0,16},{16,32},{32,48},{48,64},{64,80},{80,96},{96,112},{112,128},... | collective-permute-start | bytes 393224 | tf_op jit(solution)/shard_map/while/body/eval_jaxpr/ppermute | solution.py:12
  257.2 7.5 %collective-permute-start = (bf16[8,64,128]{2,1,0:T(8,128)(2,1)S(1)}, bf16[8,64,128]{2,1,0:T(8,128)(2,1)S(1)}, u32[]{:S(2)}, u32[]{:S(2)}) collective-permute-start(bf16[8,64,128]{2,1,0:T(8,128)(2,1)S(1)} %get-tuple-element.332), channel_id=1, source_target_pairs={{0,16},{16,32},{32,48},{48,64},{64,80},{80,96},{96,112},{112,128},... | collective-permute-start | bytes 393224 | tf_op jit(solution)/shard_map/while/body/eval_jaxpr/ppermute | solution.py:12
  265.4 7.5 %collective-permute-start = (bf16[8,64,128]{2,1,0:T(8,128)(2,1)S(1)}, bf16[8,64,128]{2,1,0:T(8,128)(2,1)S(1)}, u32[]{:S(2)}, u32[]{:S(2)}) collective-permute-start(bf16[8,64,128]{2,1,0:T(8,128)(2,1)S(1)} %get-tuple-element.332), channel_id=1, source_target_pairs={{0,16},{16,32},{32,48},{48,64},{64,80},{80,96},{96,112},{112,128},... | collective-permute-start | bytes 393224 | tf_op jit(solution)/shard_map/while/body/eval_jaxpr/ppermute | solution.py:12
  273.6 7.5 %collective-permute-start = (bf16[8,64,128]{2,1,0:T(8,128)(2,1)S(1)}, bf16[8,64,128]{2,1,0:T(8,128)(2,1)S(1)}, u32[]{:S(2)}, u32[]{:S(2)}) collective-permute-start(bf16[8,64,128]{2,1,0:T(8,128)(2,1)S(1)} %get-tuple-element.332), channel_id=1, source_target_pairs={{0,16},{16,32},{32,48},{48,64},{64,80},{80,96},{96,112},{112,128},... | collective-permute-start | bytes 393224 | tf_op jit(solution)/shard_map/while/body/eval_jaxpr/ppermute | solution.py:12
  281.8 7.5 %collective-permute-start = (bf16[8,64,128]{2,1,0:T(8,128)(2,1)S(1)}, bf16[8,64,128]{2,1,0:T(8,128)(2,1)S(1)}, u32[]{:S(2)}, u32[]{:S(2)}) collective-permute-start(bf16[8,64,128]{2,1,0:T(8,128)(2,1)S(1)} %get-tuple-element.332), channel_id=1, source_target_pairs={{0,16},{16,32},{32,48},{48,64},{64,80},{80,96},{96,112},{112,128},... | collective-permute-start | bytes 393224 | tf_op jit(solution)/shard_map/while/body/eval_jaxpr/ppermute | solution.py:12
  290.1 7.5 %collective-permute-start = (bf16[8,64,128]{2,1,0:T(8,128)(2,1)S(1)}, bf16[8,64,128]{2,1,0:T(8,128)(2,1)S(1)}, u32[]{:S(2)}, u32[]{:S(2)}) collective-permute-start(bf16[8,64,128]{2,1,0:T(8,128)(2,1)S(1)} %get-tuple-element.332), channel_id=1, source_target_pairs={{0,16},{16,32},{32,48},{48,64},{64,80},{80,96},{96,112},{112,128},... | collective-permute-start | bytes 393224 | tf_op jit(solution)/shard_map/while/body/eval_jaxpr/ppermute | solution.py:12
  298.3 7.5 %collective-permute-start = (bf16[8,64,128]{2,1,0:T(8,128)(2,1)S(1)}, bf16[8,64,128]{2,1,0:T(8,128)(2,1)S(1)}, u32[]{:S(2)}, u32[]{:S(2)}) collective-permute-start(bf16[8,64,128]{2,1,0:T(8,128)(2,1)S(1)} %get-tuple-element.332), channel_id=1, source_target_pairs={{0,16},{16,32},{32,48},{48,64},{64,80},{80,96},{96,112},{112,128},... | collective-permute-start | bytes 393224 | tf_op jit(solution)/shard_map/while/body/eval_jaxpr/ppermute | solution.py:12
  306.5 7.5 %collective-permute-start = (bf16[8,64,128]{2,1,0:T(8,128)(2,1)S(1)}, bf16[8,64,128]{2,1,0:T(8,128)(2,1)S(1)}, u32[]{:S(2)}, u32[]{:S(2)}) collective-permute-start(bf16[8,64,128]{2,1,0:T(8,128)(2,1)S(1)} %get-tuple-element.332), channel_id=1, source_target_pairs={{0,16},{16,32},{32,48},{48,64},{64,80},{80,96},{96,112},{112,128},... | collective-permute-start | bytes 393224 | tf_op jit(solution)/shard_map/while/body/eval_jaxpr/ppermute | solution.py:12
  314.7 7.5 %collective-permute-start = (bf16[8,64,128]{2,1,0:T(8,128)(2,1)S(1)}, bf16[8,64,128]{2,1,0:T(8,128)(2,1)S(1)}, u32[]{:S(2)}, u32[]{:S(2)}) collective-permute-start(bf16[8,64,128]{2,1,0:T(8,128)(2,1)S(1)} %get-tuple-element.332), channel_id=1, source_target_pairs={{0,16},{16,32},{32,48},{48,64},{64,80},{80,96},{96,112},{112,128},... | collective-permute-start | bytes 393224 | tf_op jit(solution)/shard_map/while/body/eval_jaxpr/ppermute | solution.py:12
  322.9 7.5 %collective-permute-start = (bf16[8,64,128]{2,1,0:T(8,128)(2,1)S(1)}, bf16[8,64,128]{2,1,0:T(8,128)(2,1)S(1)}, u32[]{:S(2)}, u32[]{:S(2)}) collective-permute-start(bf16[8,64,128]{2,1,0:T(8,128)(2,1)S(1)} %get-tuple-element.332), channel_id=1, source_target_pairs={{0,16},{16,32},{32,48},{48,64},{64,80},{80,96},{96,112},{112,128},... | collective-permute-start | bytes 393224 | tf_op jit(solution)/shard_map/while/body/eval_jaxpr/ppermute | solution.py:12
  331.1 7.5 %collective-permute-start = (bf16[8,64,128]{2,1,0:T(8,128)(2,1)S(1)}, bf16[8,64,128]{2,1,0:T(8,128)(2,1)S(1)}, u32[]{:S(2)}, u32[]{:S(2)}) collective-permute-start(bf16[8,64,128]{2,1,0:T(8,128)(2,1)S(1)} %get-tuple-element.332), channel_id=1, source_target_pairs={{0,16},{16,32},{32,48},{48,64},{64,80},{80,96},{96,112},{112,128},... | collective-permute-start | bytes 393224 | tf_op jit(solution)/shard_map/while/body/eval_jaxpr/ppermute | solution.py:12
  339.4 7.5 %collective-permute-start = (bf16[8,64,128]{2,1,0:T(8,128)(2,1)S(1)}, bf16[8,64,128]{2,1,0:T(8,128)(2,1)S(1)}, u32[]{:S(2)}, u32[]{:S(2)}) collective-permute-start(bf16[8,64,128]{2,1,0:T(8,128)(2,1)S(1)} %get-tuple-element.332), channel_id=1, source_target_pairs={{0,16},{16,32},{32,48},{48,64},{64,80},{80,96},{96,112},{112,128},... | collective-permute-start | bytes 393224 | tf_op jit(solution)/shard_map/while/body/eval_jaxpr/ppermute | solution.py:12
  347.6 7.5 %collective-permute-start = (bf16[8,64,128]{2,1,0:T(8,128)(2,1)S(1)}, bf16[8,64,128]{2,1,0:T(8,128)(2,1)S(1)}, u32[]{:S(2)}, u32[]{:S(2)}) collective-permute-start(bf16[8,64,128]{2,1,0:T(8,128)(2,1)S(1)} %get-tuple-element.332), channel_id=1, source_target_pairs={{0,16},{16,32},{32,48},{48,64},{64,80},{80,96},{96,112},{112,128},... | collective-permute-start | bytes 393224 | tf_op jit(solution)/shard_map/while/body/eval_jaxpr/ppermute | solution.py:12
  355.8 7.5 %collective-permute-start = (bf16[8,64,128]{2,1,0:T(8,128)(2,1)S(1)}, bf16[8,64,128]{2,1,0:T(8,128)(2,1)S(1)}, u32[]{:S(2)}, u32[]{:S(2)}) collective-permute-start(bf16[8,64,128]{2,1,0:T(8,128)(2,1)S(1)} %get-tuple-element.332), channel_id=1, source_target_pairs={{0,16},{16,32},{32,48},{48,64},{64,80},{80,96},{96,112},{112,128},... | collective-permute-start | bytes 393224 | tf_op jit(solution)/shard_map/while/body/eval_jaxpr/ppermute | solution.py:12
  366.8 2.2 copy-start
  366.8 3.5 copy-start.1
  366.8 3.5 copy-start.7
where the time goes:
time: 414 us; the launch traced here: 409 us
  local copies, waits for them, and re-layouts  141 us (34%)
  starting transfers between devices  107 us (26%)
  waiting for transfers between devices  60 us (14%)
  matrix products  40 us (10%)
  blocking collectives  32 us (8%)
  other arithmetic  27.9 us (7%)
    dynamic_update_slice x16, local copies, waits for them, and re-layouts, group_scan(): final_state, outputs = lax.scan(block_step, state_start, inputs)  106 us
    ppermute x15, starting transfers between devices, from_behind(): return lax.ppermute(block, axis, route)  85.7 us
    all_to_all x1, blocking collectives, per_device(): lax.all_to_all(y_local, 'head', split_axis=0, concat_axis=1, tiled=True)  32 us
    ppermute x15, waiting for transfers between devices, from_behind(): return lax.ppermute(block, axis, route)  28.9 us
    all_to_all x1, waiting for transfers between devices, per_device(): lax.all_to_all(x_split, 'head', split_axis=1, concat_axis=0, tiled=True)  18.9 us
    unnamed x29, local copies, waits for them, and re-layouts  14.8 us
    dot_general x8, matrix products, block_step(): jnp.einsum('ijh,jhp->ihp', weights, x_block, preferred_element_type=jnp.f...  14.1 us
    dot_general x8, matrix products, block_step(): jnp.einsum('jhn,jhp->hpn', b_scaled, x_block, preferred_element_type=jnp....  11.9 us
  transfers between devices with their start and end apart: 19, of which 18 were waited for; matrix products, arithmetic and copies ran while one was open for 6% of the time, Pallas kernels for 0%

commit v1 on v0

v1 whole, which is shorter than its diff:
```python
import functools

import jax
import jax.numpy as jnp
from jax import lax
from jax.experimental import pallas as pl
from jax.experimental.pallas import tpu as pltpu
from jax.sharding import PartitionSpec as P

MESH = pl.DeviceIdType.MESH
BF, F32 = jnp.bfloat16, jnp.float32
LOG2E = 1.4426950408889634
ROWS = 128
HEADS, GROUPS, STATE, WIDTH = 128, 8, 128, 64
PER = HEADS // GROUPS
GCOLS = PER * WIDTH
SHARDS = 16
OWN = HEADS // SHARDS * WIDTH
PIECES = 2
COLS = OWN // PIECES
HALF = COLS // 2
XS, YS, ZS = 4, 4, 8
HI = lax.Precision.HIGHEST


def dot(a, b, dims=((1,), (0,)), precision=None):
    return lax.dot_general(a, b, (dims, ((), ())), precision=precision, preferred_element_type=F32)


def two_parts(a):
    hi = a.astype(BF)
    lo = (a - hi.astype(F32)).astype(BF)
    return jnp.concatenate([hi, lo], axis=1)


def iota(shape, dim):
    return lax.broadcasted_iota(jnp.int32, shape, dim)


def kernel(
    x_hbm, b_hbm, c_hbm, dt_ref, rate_ref, bias_ref, skip_ref, y_hbm,
    xv, bv, cv, bg, cg, spread, end_parts, in_parts, skip_parts, cum_cols, cum_rows, dt_rows,
    s_out, s_in, p_out, p_in, acc, ew, yv,
    log_own, log_all, shard_own, shard_all, pair_out, pair_in, zsum_own, zsum_in, back_out, back_in,
    load_sem, b_sem, y_sem, s_send, s_recv, p_send, p_recv, log_send, log_recv,
    shard_send, shard_recv, core_send, core_recv, z_send, z_recv, back_send, back_recv,
):
    ctx, me = lax.axis_index("ctx"), lax.axis_index("head")
    z, core = ctx // 2, lax.rem(ctx, 2)
    mx, my = me // YS, lax.rem(me, YS)
    other = z * 2 + 1 - core

    def peer(i, sign):
        o = lax.rem(i * 7, SHARDS)
        px = lax.rem(mx + XS + sign * (o // YS), XS)
        py = lax.rem(my + YS + sign * lax.rem(o, YS), YS)
        return px * YS + py

    def remote(src, dst, send, recv, c, h):
        return pltpu.make_async_remote_copy(
            src_ref=src, dst_ref=dst, send_sem=send, recv_sem=recv, device_id=(c, h), device_id_type=MESH
        )

    def log_copy(to, slot):
        return remote(log_own, log_all.at[slot], log_send.at[to], log_recv.at[slot], ctx, to)

    def s_copy(p, to, slot):
        return remote(s_out.at[p, to], s_in.at[p, slot], s_send.at[p, to], s_recv.at[p, slot], ctx, to)

    def p_copy(p, to, slot):
        return remote(p_out.at[p, to], p_in.at[p, slot], p_send.at[p, to], p_recv.at[p, slot], ctx, to)

    def shard_core_copy():
        return remote(shard_own.at[core], shard_own.at[core], shard_send.at[ZS], shard_recv.at[ZS], other, me)

    def shard_core_wait():
        return remote(shard_own.at[1 - core], shard_own.at[1 - core], shard_send.at[ZS], shard_recv.at[ZS], other, me)

    def shard_copy(to, slot):
        return remote(shard_own, shard_all.at[slot], shard_send.at[to], shard_recv.at[slot], to * 2 + core, me)

    def z_copy(p, to, slot):
        return remote(zsum_own.at[p], zsum_in.at[p, slot], z_send.at[p, to], z_recv.at[p, slot], to * 2 + core, me)

    def pair_copy(p):
        return remote(pair_out.at[p], pair_in.at[p], core_send.at[p], core_recv.at[p], other, me)

    def back_copy(p):
        return remote(back_out.at[p], back_in.at[p], back_send.at[p], back_recv.at[p], other, me)

    def x_load(g):
        cols = pl.ds(pl.multiple_of(g * GCOLS, GCOLS), GCOLS)
        return pltpu.make_async_copy(x_hbm.at[:, cols], xv.at[:, cols], load_sem.at[g])

    b_load = pltpu.make_async_copy(b_hbm, bv, b_sem.at[0])
    c_load = pltpu.make_async_copy(c_hbm, cv, b_sem.at[1])
    b_load.start()
    for g in range(GROUPS):
        x_load(g).start()
    c_load.start()

    barrier = pltpu.get_barrier_semaphore()

    def greet_head(i, carry):
        pl.semaphore_signal(barrier, inc=1, device_id=(ctx, peer(i, 1)), device_id_type=MESH)
        return carry

    lax.fori_loop(1, SHARDS, greet_head, 0)

    def greet_z(d, carry):
        pl.semaphore_signal(
            barrier, inc=1, device_id=(lax.rem(z + d, ZS) * 2 + core, me), device_id_type=MESH
        )
        return carry

    lax.fori_loop(1, ZS, greet_z, 0)
    pl.semaphore_signal(barrier, inc=1, device_id=(other, me), device_id_type=MESH)

    raw = dt_ref[...].astype(F32) + bias_ref[...]
    step = jnp.maximum(raw, 0.0) + jnp.log1p(jnp.exp(-jnp.abs(raw)))
    log_decay = -rate_ref[...] * step
    lower = iota((ROWS, ROWS), 0) >= iota((ROWS, ROWS), 1)
    within = dot(lower.astype(F32), log_decay, precision=HI)
    total = within[ROWS - 1 : ROWS, :]
    log_own[...] = jnp.broadcast_to(total, (8, HEADS))
    end_weight = two_parts(jnp.exp(total - within) * step)
    in_weight = two_parts(jnp.exp(within))
    skip_hl = two_parts(jnp.broadcast_to(skip_ref[...], (16, HEADS)))
    scaled = within * LOG2E
    scaled_t = jnp.transpose(scaled)
    step_t = jnp.transpose(step)
    for g in range(GROUPS):
        lo, hi = g * PER, (g + 1) * PER
        for ref, value in ((end_parts, end_weight), (in_parts, in_weight), (skip_parts, skip_hl)):
            ref[g] = jnp.concatenate([value[:, lo:hi], value[:, HEADS + lo : HEADS + hi]], axis=1)
        cum_cols[g] = scaled[:, lo:hi]
        cum_rows[g] = scaled_t[lo:hi, :]
        dt_rows[g] = step_t[lo:hi, :]
    spread[...] = (lax.rem(iota((2 * PER, GCOLS), 0), PER) == iota((2 * PER, GCOLS), 1) // WIDTH).astype(BF)

    order_row, order_col = iota((256, 256), 0), iota((256, 256), 1)
    order = (order_col == lax.rem(order_row, 32) * GROUPS + order_row // 32).astype(BF)

    def regroup(src, dst):
        for strip in range(ROWS // 32):
            part = dot(order, src[strip * 256 : (strip + 1) * 256, :]).astype(BF)
            for g in range(GROUPS):
                dst[g, strip * 32 : (strip + 1) * 32, :] = part[g * 32 : (g + 1) * 32, :]

    b_load.wait()
    regroup(bv, bg)

    def own_state(g, carry):
        x_load(g).wait()
        cols = pl.ds(pl.multiple_of(g * GCOLS, GCOLS), GCOLS)
        weight = dot(end_parts[g], spread[...])
        xs = (xv[:, cols].astype(F32) * weight).astype(BF)
        value = dot(bg[g], xs, ((0,), (0,))).astype(BF)
        for a in range(2):
            for p in range(PIECES):
                at = a * OWN + p * COLS
                s_out[p, 2 * g + a] = value[:, at : at + COLS]
        return carry

    lax.fori_loop(0, GROUPS, own_state, 0)

    pl.semaphore_wait(barrier, SHARDS - 1 + ZS - 1 + 1)

    def send_logs(i, carry):
        log_copy(peer(i, 1), me).start()
        return carry

    lax.fori_loop(1, SHARDS, send_logs, 0)
    for p in range(PIECES):

        def send_s(i, carry):
            s_copy(p, peer(i, 1), me).start()
            return carry

        lax.fori_loop(1, SHARDS, send_s, 0)

    c_load.wait()
    regroup(cv, cg)

    lane = iota((ROWS, 2 * WIDTH), 1)

    def inside(g, carry):
        scores = jnp.where(lower, dot(cg[g], bg[g], ((1,), (1,))), 0.0)
        skip = dot(skip_parts[g], spread[...])
        col, row, dts = cum_cols[g], cum_rows[g], dt_rows[g]
        for pair in range(PER // 2):
            parts = []
            for h in (2 * pair, 2 * pair + 1):
                span = col[:, h : h + 1] - row[h : h + 1, :]
                decay = jnp.exp2(jnp.minimum(span, 0.0))
                parts.append((scores * decay * dts[h : h + 1, :]).astype(BF))
            at = pair * 2 * WIDTH
            x2 = xv[:, pl.ds(pl.multiple_of(g * GCOLS + at, 2 * WIDTH), 2 * WIDTH)]
            zero = jnp.zeros_like(x2)
            blocks = jnp.concatenate(
                [jnp.where(lane < WIDTH, x2, zero), jnp.where(lane < WIDTH, zero, x2)], axis=0
            )
            value = dot(jnp.concatenate(parts, axis=1), blocks)
            value = value + skip[0:1, at : at + 2 * WIDTH] * x2.astype(F32)
            acc[2 * g + at // OWN, :, at % OWN : at % OWN + 2 * WIDTH] = value
        weight = dot(in_parts[g], spread[...])
        ew[2 * g] = weight[:, :OWN]
        ew[2 * g + 1] = weight[:, OWN:]
        return carry

    lax.fori_loop(0, 3, inside, 0)

    def logs_in(i, carry):
        src = peer(i, -1)
        log_copy(src, src).wait_recv()
        return carry

    lax.fori_loop(1, SHARDS, logs_in, 0)
    log_all[me] = log_own[...]
    logs = log_all[:, 0, :]
    shard_log = jnp.sum(logs, axis=0, keepdims=True)
    shard_own[core] = jnp.broadcast_to(shard_log, (8, HEADS))
    shard_core_copy().start()
    later = (iota((SHARDS, SHARDS), 1) > iota((SHARDS, SHARDS), 0)).astype(F32)
    to_end = dot(later, logs, precision=HI)
    mine = (iota((HEADS, OWN), 0) == me * (HEADS // SHARDS) + iota((HEADS, OWN), 1) // WIDTH).astype(F32)
    chunk_decay = jnp.exp(dot(logs, mine, precision=HI))
    end_decay = jnp.exp(dot(to_end, mine, precision=HI))

    lax.fori_loop(3, 4, inside, 0)
    shard_core_wait().wait_recv()

    def send_shard(d, carry):
        shard_copy(lax.rem(z + d, ZS), z).start()
        return carry

    lax.fori_loop(1, ZS, send_shard, 0)
    lax.fori_loop(4, GROUPS, inside, 0)

    def shard_wait(d, carry):
        src = lax.rem(z + ZS - d, ZS)
        shard_copy(src, src).wait_recv()
        return carry

    lax.fori_loop(1, ZS, shard_wait, 0)
    shard_all[z] = shard_own[...]
    shard_logs = shard_all[:, :, 0, :]
    pair_logs = shard_logs[:, 0, :] + shard_logs[:, 1, :]
    zi, zj = iota((ZS, ZS), 0), iota((ZS, ZS), 1)
    between = ((zj > zi) & (zj < z)).astype(F32)
    z_logs = dot(between, pair_logs, precision=HI)
    z_weight = jnp.where(iota((ZS, OWN), 0) < z, jnp.exp(dot(z_logs, mine, precision=HI)), 0.0)
    pair_decay = jnp.exp(dot(shard_all[z, :, 0, :], mine, precision=HI))

    def mine_half(value):
        return jnp.where(core == 0, value[:, :HALF], value[:, HALF:])

    def gather(p):
        cols = slice(p * COLS, (p + 1) * COLS)

        def s_wait(i, carry):
            src = peer(i, -1)
            s_copy(p, src, src).wait_recv()
            return carry

        lax.fori_loop(1, SHARDS, s_wait, 0)
        s_in[p, me] = s_out[p, me]
        value = s_in[p, SHARDS - 1].astype(F32)
        for j in range(SHARDS - 1):
            value += end_decay[j : j + 1, cols] * s_in[p, j].astype(F32)
        keep = mine_half(value)
        pair_out[p] = jnp.where(core == 0, value[:, HALF:], value[:, :HALF]).astype(BF)
        pair_copy(p).start()
        pair_copy(p).wait_recv()
        theirs = pair_in[p].astype(F32)
        first = jnp.where(core == 0, keep, theirs)
        second = jnp.where(core == 0, theirs, keep)
        decay = mine_half(pair_decay[1:2, cols])
        zsum_own[p] = (first * decay + second).astype(BF)

        def z_start(d, carry):
            z_copy(p, lax.rem(z + d, ZS), z).start()
            return carry

        lax.fori_loop(1, ZS, z_start, 0)
        return first

    def give_back(p, first):
        cols = slice(p * COLS, (p + 1) * COLS)

        def z_wait(d, carry):
            src = lax.rem(z + ZS - d, ZS)
            z_copy(p, src, src).wait_recv()
            return carry

        lax.fori_loop(1, ZS, z_wait, 0)
        zsum_in[p, z] = zsum_own[p]
        weight = mine_half(z_weight[:, cols])
        before = jnp.zeros((STATE, HALF), F32)
        for j in range(ZS - 1):
            before += weight[j : j + 1, :] * zsum_in[p, j].astype(F32)
        after = before * mine_half(pair_decay[0:1, cols]) + first
        back_out[p] = jnp.where(core == 0, after, before).astype(BF)
        back_copy(p).start()
        back_copy(p).wait_recv()
        keep = jnp.where(core == 0, before, after)
        theirs = back_in[p].astype(F32)
        state = jnp.where(
            core == 0, jnp.concatenate([keep, theirs], axis=1), jnp.concatenate([theirs, keep], axis=1)
        )
        for j in range(SHARDS):
            p_out[p, j] = state.astype(BF)
            if j < SHARDS - 1:
                state = state * chunk_decay[j : j + 1, cols] + s_in[p, j].astype(F32)
        p_in[p, me] = p_out[p, me]

        def p_start(i, carry):
            p_copy(p, peer(i, 1), me).start()
            return carry

        lax.fori_loop(1, SHARDS, p_start, 0)

    def y_store(k):
        cols = pl.ds(pl.multiple_of(k * OWN, OWN), OWN)
        return pltpu.make_async_copy(yv.at[k], y_hbm.at[:, cols], y_sem.at[k])

    def finish(p, k):
        across = dot(cg[k // 2], p_in[p, k])
        cols = slice(p * COLS, (p + 1) * COLS)
        yv[k, :, cols] = (acc[k, :, cols] + ew[k, :, cols] * across).astype(BF)
        if p == PIECES - 1:
            y_store(k).start()

    firsts = {}
    firsts[0] = gather(0)
    give_back(0, firsts[0])
    firsts[1] = gather(1)
    give_back(1, firsts[1])
    for p in range(PIECES):
        finish(p, me)

        def p_wait(i, carry):
            src = peer(i, -1)
            p_copy(p, src, src).wait_recv()
            finish(p, src)
            return carry

        lax.fori_loop(1, SHARDS, p_wait, 0)

    def sent_head(i, carry):
        to = peer(i, 1)
        log_copy(to, me).wait_send()
        for p in range(PIECES):
            s_copy(p, to, me).wait_send()
            p_copy(p, to, me).wait_send()
        return carry

    lax.fori_loop(1, SHARDS, sent_head, 0)

    def sent_z(d, carry):
        to = lax.rem(z + d, ZS)
        shard_copy(to, z).wait_send()
        for p in range(PIECES):
            z_copy(p, to, z).wait_send()
        return carry

    lax.fori_loop(1, ZS, sent_z, 0)
    shard_core_copy().wait_send()
    for p in range(PIECES):
        pair_copy(p).wait_send()
        back_copy(p).wait_send()

    def stored(k, carry):
        y_store(k).wait()
        return carry

    lax.fori_loop(0, SHARDS, stored, 0)


def per_device(x_in, b_in, c_in, dt_raw, decay_rate, dt_bias, skip_gain):
    vmem, dma = pltpu.VMEM, pltpu.SemaphoreType.DMA
    any_spec, vmem_spec = pl.BlockSpec(memory_space=pl.ANY), pl.BlockSpec(memory_space=pltpu.VMEM)
    return pl.pallas_call(
        kernel,
        name="scan",
        out_shape=jax.ShapeDtypeStruct((ROWS, HEADS * WIDTH), BF),
        in_specs=[any_spec] * 3 + [vmem_spec] * 4,
        out_specs=any_spec,
        scratch_shapes=[
            vmem((ROWS, HEADS * WIDTH), BF),
            vmem((ROWS * GROUPS, STATE), BF),
            vmem((ROWS * GROUPS, STATE), BF),
            vmem((GROUPS, ROWS, STATE), BF),
            vmem((GROUPS, ROWS, STATE), BF),
            vmem((2 * PER, GCOLS), BF),
            vmem((GROUPS, ROWS, 2 * PER), BF),
            vmem((GROUPS, ROWS, 2 * PER), BF),
            vmem((GROUPS, 16, 2 * PER), BF),
            vmem((GROUPS, ROWS, PER), F32),
            vmem((GROUPS, PER, ROWS), F32),
            vmem((GROUPS, PER, ROWS), F32),
            vmem((PIECES, SHARDS, STATE, COLS), BF),
            vmem((PIECES, SHARDS, STATE, COLS), BF),
            vmem((PIECES, SHARDS, STATE, COLS), BF),
            vmem((PIECES, SHARDS, STATE, COLS), BF),
            vmem((SHARDS, ROWS, OWN), F32),
            vmem((SHARDS, ROWS, OWN), F32),
            vmem((SHARDS, ROWS, OWN), BF),
            vmem((8, HEADS), F32),
            vmem((SHARDS, 8, HEADS), F32),
            vmem((2, 8, HEADS), F32),
            vmem((ZS, 2, 8, HEADS), F32),
            vmem((PIECES, STATE, HALF), BF),
            vmem((PIECES, STATE, HALF), BF),
            vmem((PIECES, STATE, HALF), BF),
            vmem((PIECES, ZS, STATE, HALF), BF),
            vmem((PIECES, STATE, HALF), BF),
            vmem((PIECES, STATE, HALF), BF),
            dma((GROUPS,)),
            dma((2,)),
            dma((SHARDS,)),
            dma((PIECES, SHARDS)),
            dma((PIECES, SHARDS)),
            dma((PIECES, SHARDS)),
            dma((PIECES, SHARDS)),
            dma((SHARDS,)),
            dma((SHARDS,)),
            dma((ZS + 1,)),
            dma((ZS + 1,)),
            dma((PIECES,)),
            dma((PIECES,)),
            dma((PIECES, ZS)),
            dma((PIECES, ZS)),
            dma((PIECES,)),
            dma((PIECES,)),
        ],
        compiler_params=pltpu.CompilerParams(
            collective_id=0, has_side_effects=True, vmem_limit_bytes=48 * 1024 * 1024
        ),
    )(
        x_in,
        b_in.reshape(ROWS * GROUPS, STATE),
        c_in.reshape(ROWS * GROUPS, STATE),
        dt_raw,
        decay_rate.reshape(1, HEADS),
        dt_bias.reshape(1, HEADS),
        skip_gain.reshape(1, HEADS),
    )


def solution(mesh):
    rows = ("ctx", "head")
    in_specs = (P(rows, None), P(rows, None, None), P(rows, None, None), P(rows, None), P(), P(), P())
    return jax.shard_map(
        per_device, mesh=mesh, in_specs=in_specs, out_specs=P(rows, None), check_vma=False
    )
```

time: 414 us -> 79.1 us (0.19)
  the two profiles are of different devices: /device:TPU:97 before, /device:TPU:1 now
where the time goes in v1:
time: 79.1 us; the launch traced here: 78.8 us
  Pallas kernels  71.3 us (90%)
  local copies, waits for them, and re-layouts  7.53 us (10%)
    pallas_call x1, Pallas kernels, per_device(): pl.pallas_call(kernel, name='scan', out_shape=jax.ShapeDtypeStruct((ROWS,...  71.3 us
    unnamed x15, local copies, waits for them, and re-layouts  7.53 us

profile of v1, /device:TPU:1, one launch (start us, length us, event | category | flops | bytes accessed | tf_op | source)
XLA Modules:
  0.0 78.8 jit_solution(3819527685542304182)
XLA Ops:
  0.0 0.0 copy-start
  0.0 1.6 %copy-done = bf16[128,8192]{1,0:T(8,128)(2,1)S(1)} copy-done((bf16[128,8192]{1,0:T(8,128)(2,1)S(1)}, bf16[128,8192]{1,0:T(8,128)(2,1)}, u32[]{:S(2)}) %copy-start) | copy-done | bytes 2097176
  1.6 0.0 copy-start.1
  1.6 0.9 %copy-done.1 = bf16[128,8,128]{2,1,0:T(8,128)(2,1)S(1)} copy-done((bf16[128,8,128]{2,1,0:T(8,128)(2,1)S(1)}, bf16[128,8,128]{2,1,0:T(8,128)(2,1)}, u32[]{:S(2)}) %copy-start.1) | copy-done | bytes 262168
  2.5 0.0 copy-start.2
  2.5 0.9 %copy-done.2 = bf16[128,8,128]{2,1,0:T(8,128)(2,1)S(1)} copy-done((bf16[128,8,128]{2,1,0:T(8,128)(2,1)S(1)}, bf16[128,8,128]{2,1,0:T(8,128)(2,1)}, u32[]{:S(2)}) %copy-start.2) | copy-done | bytes 262168
  3.5 0.0 copy-start.3
  3.5 0.8 copy-done.3
  4.3 0.0 copy-start.4
  4.3 0.7 copy-done.4
  4.9 0.0 copy-start.5
  4.9 0.7 copy-done.5
  5.6 0.0 copy-start.6
  5.6 0.7 copy-done.6
  6.2 71.3 %scan.1 = bf16[128,8192]{1,0:T(8,128)(2,1)S(1)} custom-call(bf16[128,8192]{1,0:T(8,128)(2,1)S(1)} %copy-done, bf16[1024,128]{1,0:T(8,128)(2,1)S(1)} %bitcast.5, bf16[1024,128]{1,0:T(8,128)(2,1)S(1)} %bitcast.6, bf16[128,128]{1,0:T(8,128)(2,1)S(1)} %copy-done.3, f32[1,128]{1,0:T(1,128)S(1)} %bitcast.7, f32[1,128]{1,0:T(1,128)S(1)} %bitcast.8, ...), custom_call_target="tpu_custom_call" | custom-call | tf_op jit(solution)/shard_map/scan/pallas_call | solution.py:383
  77.5 1.3 %copy.9 = bf16[128,8192]{1,0:T(8,128)(2,1)} copy(bf16[128,8192]{1,0:T(8,128)(2,1)S(1)} %scan.1) | data formatting | bytes 4194304
Async XLA Ops:
  0.0 1.6 %copy-start = (bf16[128,8192]{1,0:T(8,128)(2,1)S(1)}, bf16[128,8192]{1,0:T(8,128)(2,1)}, u32[]{:S(2)}) copy-start(bf16[128,8192]{1,0:T(8,128)(2,1)} %x_hbm.1) | copy-start | bytes 6291460
  1.6 0.9 %copy-start.1 = (bf16[128,8,128]{2,1,0:T(8,128)(2,1)S(1)}, bf16[128,8,128]{2,1,0:T(8,128)(2,1)}, u32[]{:S(2)}) copy-start(bf16[128,8,128]{2,1,0:T(8,128)(2,1)} %param.8) | copy-start | bytes 786436
  2.5 0.9 %copy-start.2 = (bf16[128,8,128]{2,1,0:T(8,128)(2,1)S(1)}, bf16[128,8,128]{2,1,0:T(8,128)(2,1)}, u32[]{:S(2)}) copy-start(bf16[128,8,128]{2,1,0:T(8,128)(2,1)} %param.9) | copy-start | bytes 786436
  3.5 0.8 copy-start.3
  4.3 0.7 copy-start.4
  4.9 0.7 copy-start.5
  5.6 0.7 copy-start.6

commit v2 on v1

--- a/solution.py
+++ b/solution.py
@@ -16,9 +16,9 @@
 GCOLS = PER * WIDTH
 SHARDS = 16
 OWN = HEADS // SHARDS * WIDTH
-PIECES = 2
+PIECES = 4
 COLS = OWN // PIECES
-HALF = COLS // 2
+HALF = STATE // 2
 XS, YS, ZS = 4, 4, 8
 HI = lax.Precision.HIGHEST
 
@@ -38,11 +38,12 @@
 
 
 def kernel(
-    x_hbm, b_hbm, c_hbm, dt_ref, rate_ref, bias_ref, skip_ref, y_hbm,
-    xv, bv, cv, bg, cg, spread, end_parts, in_parts, skip_parts, cum_cols, cum_rows, dt_rows,
-    s_out, s_in, p_out, p_in, acc, ew, yv,
+    x_hbm, b_hbm, c_hbm, dt_hbm, rate_hbm, bias_hbm, skip_hbm, y_ref,
+    dt_ref, rate_ref, bias_ref, skip_ref, xv, bv, cv, bg, cg, spread, end_parts, in_parts, skip_parts, cum_cols, cum_rows, dt_rows,
+    s_out, s_in, p_out, p_in, acc, ew,
     log_own, log_all, shard_own, shard_all, pair_out, pair_in, zsum_own, zsum_in, back_out, back_in,
-    load_sem, b_sem, y_sem, s_send, s_recv, p_send, p_recv, log_send, log_recv,
+    end_rows, z_rows, total_state, before_state, firsts,
+    load_sem, b_sem, s_send, s_recv, p_send, p_recv, log_send, log_recv,
     shard_send, shard_recv, core_send, core_recv, z_send, z_recv, back_send, back_recv,
 ):
     ctx, me = lax.axis_index("ctx"), lax.axis_index("head")
@@ -94,11 +95,24 @@
 
     b_load = pltpu.make_async_copy(b_hbm, bv, b_sem.at[0])
     c_load = pltpu.make_async_copy(c_hbm, cv, b_sem.at[1])
+    small = [
+        pltpu.make_async_copy(src, dst, b_sem.at[2 + i])
+        for i, (src, dst) in enumerate(
+            ((dt_hbm, dt_ref), (rate_hbm, rate_ref), (bias_hbm, bias_ref), (skip_hbm, skip_ref))
+        )
+    ]
+    for load in small:
+        load.start()
     b_load.start()
-    for g in range(GROUPS):
-        x_load(g).start()
+
+    def start_load(i, carry):
+        x_load(lax.rem(me // 2 + 1 + i, GROUPS)).start()
+        return carry
+
+    lax.fori_loop(0, GROUPS, start_load, 0)
     c_load.start()
 
+    shard_all[...] = jnp.zeros_like(shard_all)
     barrier = pltpu.get_barrier_semaphore()
 
     def greet_head(i, carry):
@@ -107,15 +121,15 @@
 
     lax.fori_loop(1, SHARDS, greet_head, 0)
 
-    def greet_z(d, carry):
-        pl.semaphore_signal(
-            barrier, inc=1, device_id=(lax.rem(z + d, ZS) * 2 + core, me), device_id_type=MESH
-        )
-        return carry
-
-    lax.fori_loop(1, ZS, greet_z, 0)
+    def greet_z(back, carry):
+        pl.semaphore_signal(barrier, inc=1, device_id=(back * 2 + core, me), device_id_type=MESH)
+        return carry
+
+    lax.fori_loop(0, z, greet_z, 0)
     pl.semaphore_signal(barrier, inc=1, device_id=(other, me), device_id_type=MESH)
 
+    for load in small:
+        load.wait()
     raw = dt_ref[...].astype(F32) + bias_ref[...]
     step = jnp.maximum(raw, 0.0) + jnp.log1p(jnp.exp(-jnp.abs(raw)))
     log_decay = -rate_ref[...] * step
@@ -150,7 +164,16 @@
     b_load.wait()
     regroup(bv, bg)
 
-    def own_state(g, carry):
+    pl.semaphore_wait(barrier, SHARDS - 1 + ZS - 1 - z + 1)
+
+    def send_logs(i, carry):
+        log_copy(peer(i, 1), me).start()
+        return carry
+
+    lax.fori_loop(1, SHARDS, send_logs, 0)
+
+    def own_state(i, carry):
+        g = lax.rem(me // 2 + 1 + i, GROUPS)
         x_load(g).wait()
         cols = pl.ds(pl.multiple_of(g * GCOLS, GCOLS), GCOLS)
         weight = dot(end_parts[g], spread[...])
@@ -160,18 +183,16 @@
             for p in range(PIECES):
                 at = a * OWN + p * COLS
                 s_out[p, 2 * g + a] = value[:, at : at + COLS]
+        for a in range(2):
+
+            @pl.when(2 * g + a != me)
+            def _():
+                s_copy(0, 2 * g + a, me).start()
+
         return carry
 
     lax.fori_loop(0, GROUPS, own_state, 0)
-
-    pl.semaphore_wait(barrier, SHARDS - 1 + ZS - 1 + 1)
-
-    def send_logs(i, carry):
-        log_copy(peer(i, 1), me).start()
-        return carry
-
-    lax.fori_loop(1, SHARDS, send_logs, 0)
-    for p in range(PIECES):
+    for p in range(1, PIECES):
 
         def send_s(i, carry):
             s_copy(p, peer(i, 1), me).start()
@@ -208,7 +229,7 @@
         ew[2 * g + 1] = weight[:, OWN:]
         return carry
 
-    lax.fori_loop(0, 3, inside, 0)
+    lax.fori_loop(0, 2, inside, 0)
 
     def logs_in(i, carry):
         src = peer(i, -1)
@@ -226,87 +247,85 @@
     mine = (iota((HEADS, OWN), 0) == me * (HEADS // SHARDS) + iota((HEADS, OWN), 1) // WIDTH).astype(F32)
     chunk_decay = jnp.exp(dot(logs, mine, precision=HI))
     end_decay = jnp.exp(dot(to_end, mine, precision=HI))
-
-    lax.fori_loop(3, 4, inside, 0)
+    for j in range(SHARDS):
+        end_rows[j] = jnp.broadcast_to(end_decay[j : j + 1, :], (8, OWN))
+
+    lax.fori_loop(2, 4, inside, 0)
     shard_core_wait().wait_recv()
 
-    def send_shard(d, carry):
-        shard_copy(lax.rem(z + d, ZS), z).start()
-        return carry
-
-    lax.fori_loop(1, ZS, send_shard, 0)
-    lax.fori_loop(4, GROUPS, inside, 0)
-
-    def shard_wait(d, carry):
-        src = lax.rem(z + ZS - d, ZS)
+    def send_shard(to, carry):
+        shard_copy(to, z).start()
+        return carry
+
+    lax.fori_loop(z + 1, ZS, send_shard, 0)
+
+    def shard_wait(src, carry):
         shard_copy(src, src).wait_recv()
         return carry
 
-    lax.fori_loop(1, ZS, shard_wait, 0)
+    lax.fori_loop(0, z, shard_wait, 0)
     shard_all[z] = shard_own[...]
     shard_logs = shard_all[:, :, 0, :]
     pair_logs = shard_logs[:, 0, :] + shard_logs[:, 1, :]
     zi, zj = iota((ZS, ZS), 0), iota((ZS, ZS), 1)
     between = ((zj > zi) & (zj < z)).astype(F32)
     z_logs = dot(between, pair_logs, precision=HI)
-    z_weight = jnp.where(iota((ZS, OWN), 0) < z, jnp.exp(dot(z_logs, mine, precision=HI)), 0.0)
+    z_weight = jnp.exp(dot(z_logs, mine, precision=HI))
+    for j in range(ZS):
+        z_rows[j] = jnp.broadcast_to(z_weight[j : j + 1, :], (8, OWN))
     pair_decay = jnp.exp(dot(shard_all[z, :, 0, :], mine, precision=HI))
 
-    def mine_half(value):
-        return jnp.where(core == 0, value[:, :HALF], value[:, HALF:])
+    def half(value, which):
+        return jnp.where(which == 0, value[:HALF, :], value[HALF:, :])
 
     def gather(p):
         cols = slice(p * COLS, (p + 1) * COLS)
+        s_in[p, me] = s_out[p, me]
+        total_state[...] = end_rows[me][0:1, cols] * s_in[p, me].astype(F32)
 
         def s_wait(i, carry):
             src = peer(i, -1)
             s_copy(p, src, src).wait_recv()
+            total_state[...] += end_rows[src][0:1, cols] * s_in[p, src].astype(F32)
             return carry
 
         lax.fori_loop(1, SHARDS, s_wait, 0)
-        s_in[p, me] = s_out[p, me]
-        value = s_in[p, SHARDS - 1].astype(F32)
-        for j in range(SHARDS - 1):
-            value += end_decay[j : j + 1, cols] * s_in[p, j].astype(F32)
-        keep = mine_half(value)
-        pair_out[p] = jnp.where(core == 0, value[:, HALF:], value[:, :HALF]).astype(BF)
+        value = total_state[...]
+        keep = half(value, core)
+        pair_out[p] = half(value, 1 - core).astype(BF)
         pair_copy(p).start()
         pair_copy(p).wait_recv()
         theirs = pair_in[p].astype(F32)
         first = jnp.where(core == 0, keep, theirs)
         second = jnp.where(core == 0, theirs, keep)
-        decay = mine_half(pair_decay[1:2, cols])
-        zsum_own[p] = (first * decay + second).astype(BF)
-
-        def z_start(d, carry):
-            z_copy(p, lax.rem(z + d, ZS), z).start()
-            return carry
-
-        lax.fori_loop(1, ZS, z_start, 0)
-        return first
-
-    def give_back(p, first):
+        zsum_own[p] = (first * pair_decay[1:2, cols] + second).astype(BF)
+
+        def z_start(to, carry):
+            z_copy(p, to, z).start()
+            return carry
+
+        lax.fori_loop(z + 1, ZS, z_start, 0)
+        firsts[p] = first
+
+    def give_back(p):
         cols = slice(p * COLS, (p + 1) * COLS)
-
-        def z_wait(d, carry):
-            src = lax.rem(z + ZS - d, ZS)
+        before_state[...] = jnp.zeros_like(before_state)
+
+        def z_wait(src, carry):
             z_copy(p, src, src).wait_recv()
-            return carry
-
-        lax.fori_loop(1, ZS, z_wait, 0)
-        zsum_in[p, z] = zsum_own[p]
-        weight = mine_half(z_weight[:, cols])
-        before = jnp.zeros((STATE, HALF), F32)
-        for j in range(ZS - 1):
-            before += weight[j : j + 1, :] * zsum_in[p, j].astype(F32)
-        after = before * mine_half(pair_decay[0:1, cols]) + first
+            before_state[...] += z_rows[src][0:1, cols] * zsum_in[p, src].astype(F32)
+            return carry
+
+        lax.fori_loop(0, z, z_wait, 0)
+        before = before_state[...]
+        after = before * pair_decay[0:1, cols] + firsts[p]
         back_out[p] = jnp.where(core == 0, after, before).astype(BF)
         back_copy(p).start()
         back_copy(p).wait_recv()
         keep = jnp.where(core == 0, before, after)
         theirs = back_in[p].astype(F32)
         state = jnp.where(
-            core == 0, jnp.concatenate([keep, theirs], axis=1), jnp.concatenate([theirs, keep], axis=1)
+            core == 0, jnp.concatenate([keep, theirs], axis=0), jnp.concatenate([theirs, keep], axis=0)
         )
         for j in range(SHARDS):
             p_out[p, j] = state.astype(BF)
@@ -320,32 +339,35 @@
 
         lax.fori_loop(1, SHARDS, p_start, 0)
 
-    def y_store(k):
-        cols = pl.ds(pl.multiple_of(k * OWN, OWN), OWN)
-        return pltpu.make_async_copy(yv.at[k], y_hbm.at[:, cols], y_sem.at[k])
-
     def finish(p, k):
         across = dot(cg[k // 2], p_in[p, k])
         cols = slice(p * COLS, (p + 1) * COLS)
-        yv[k, :, cols] = (acc[k, :, cols] + ew[k, :, cols] * across).astype(BF)
-        if p == PIECES - 1:
-            y_store(k).start()
-
-    firsts = {}
-    firsts[0] = gather(0)
-    give_back(0, firsts[0])
-    firsts[1] = gather(1)
-    give_back(1, firsts[1])
+        value = (acc[k, :, cols] + ew[k, :, cols] * across).astype(BF)
+        y_ref[:, pl.ds(pl.multiple_of(k * OWN + p * COLS, COLS), COLS)] = value
+
+    gather(0)
+    lax.fori_loop(4, 6, inside, 0)
+    gather(1)
+    give_back(0)
+    lax.fori_loop(6, 7, inside, 0)
+    gather(2)
+    give_back(1)
+    lax.fori_loop(7, GROUPS, inside, 0)
+    gather(3)
+    give_back(2)
+    give_back(3)
     for p in range(PIECES):
         finish(p, me)
 
         def p_wait(i, carry):
-            src = peer(i, -1)
-            p_copy(p, src, src).wait_recv()
-            finish(p, src)
-            return carry
-
-        lax.fori_loop(1, SHARDS, p_wait, 0)
+            batch = [peer(3 * i + 1 + j, -1) for j in range(3)]
+            for src in batch:
+                p_copy(p, src, src).wait_recv()
+            for src in batch:
+                finish(p, src)
+            return carry
+
+        lax.fori_loop(0, (SHARDS - 1) // 3, p_wait, 0)
 
     def sent_head(i, carry):
         to = peer(i, 1)
@@ -357,36 +379,33 @@
 
     lax.fori_loop(1, SHARDS, sent_head, 0)
 
-    def sent_z(d, carry):
-        to = lax.rem(z + d, ZS)
+    def sent_z(to, carry):
         shard_copy(to, z).wait_send()
         for p in range(PIECES):
             z_copy(p, to, z).wait_send()
         return carry
 
-    lax.fori_loop(1, ZS, sent_z, 0)
+    lax.fori_loop(z + 1, ZS, sent_z, 0)
     shard_core_copy().wait_send()
     for p in range(PIECES):
         pair_copy(p).wait_send()
         back_copy(p).wait_send()
 
-    def stored(k, carry):
-        y_store(k).wait()
-        return carry
-
-    lax.fori_loop(0, SHARDS, stored, 0)
-
 
 def per_device(x_in, b_in, c_in, dt_raw, decay_rate, dt_bias, skip_gain):
     vmem, dma = pltpu.VMEM, pltpu.SemaphoreType.DMA
-    any_spec, vmem_spec = pl.BlockSpec(memory_space=pl.ANY), pl.BlockSpec(memory_space=pltpu.VMEM)
+    any_spec = pl.BlockSpec(memory_space=pltpu.HBM)
     return pl.pallas_call(
         kernel,
         name="scan",
-        out_shape=jax.ShapeDtypeStruct((ROWS, HEADS * WIDTH), BF),
-        in_specs=[any_spec] * 3 + [vmem_spec] * 4,
-        out_specs=any_spec,
+        out_shape=pltpu.VMEM((ROWS, HEADS * WIDTH), BF),
+        in_specs=[any_spec] * 7,
+        out_specs=pl.BlockSpec(memory_space=pltpu.VMEM),
         scratch_shapes=[
+            vmem((ROWS, HEADS), BF),
+            vmem((1, HEADS), F32),
+            vmem((1, HEADS), F32),
+            vmem((1, HEADS), F32),
             vmem((ROWS, HEADS * WIDTH), BF),
             vmem((ROWS * GROUPS, STATE), BF),
             vmem((ROWS * GROUPS, STATE), BF),
@@ -405,20 +424,23 @@
             vmem((PIECES, SHARDS, STATE, COLS), BF),
             vmem((SHARDS, ROWS, OWN), F32),
             vmem((SHARDS, ROWS, OWN), F32),
-            vmem((SHARDS, ROWS, OWN), BF),
             vmem((8, HEADS), F32),
             vmem((SHARDS, 8, HEADS), F32),
             vmem((2, 8, HEADS), F32),
             vmem((ZS, 2, 8, HEADS), F32),
-            vmem((PIECES, STATE, HALF), BF),
-            vmem((PIECES, STATE, HALF), BF),
-            vmem((PIECES, STATE, HALF), BF),
-            vmem((PIECES, ZS, STATE, HALF), BF),
-            vmem((PIECES, STATE, HALF), BF),
-            vmem((PIECES, STATE, HALF), BF),
+            vmem((PIECES, HALF, COLS), BF),
+            vmem((PIECES, HALF, COLS), BF),
+            vmem((PIECES, HALF, COLS), BF),
+            vmem((PIECES, ZS, HALF, COLS), BF),
+            vmem((PIECES, HALF, COLS), BF),
+            vmem((PIECES, HALF, COLS), BF),
+            vmem((SHARDS, 8, OWN), F32),
+            vmem((ZS, 8, OWN), F32),
+            vmem((STATE, COLS), F32),
+            vmem((HALF, COLS), F32),
+            vmem((PIECES, HALF, COLS), F32),
             dma((GROUPS,)),
-            dma((2,)),
-            dma((SHARDS,)),
+            dma((6,)),
             dma((PIECES, SHARDS)),
             dma((PIECES, SHARDS)),
             dma((PIECES, SHARDS)),
@@ -435,7 +457,7 @@
             dma((PIECES,)),
         ],
         compiler_params=pltpu.CompilerParams(
-            collective_id=0, has_side_effects=True, vmem_limit_bytes=48 * 1024 * 1024
+            collective_id=0, has_side_effects=True, vmem_limit_bytes=61 * 1024 * 1024
         ),
     )(
         x_in,

time: 79.1 us -> 64.9 us (0.82)
  Pallas kernels: 71.3 us -> 63.5 us
  local copies, waits for them, and re-layouts: 7.53 us -> 1.32 us
    pallas_call x1, Pallas kernels: 71.3 us -> 63.5 us  [per_device(): pl.pallas_call(kernel, name='scan', out_shape=pltpu.VMEM((ROWS, HEADS * W...]
    unnamed x15 -> x1, local copies, waits for them, and re-layouts: 7.53 us -> 1.32 us
where the time goes in v2:
time: 64.9 us; the launch traced here: 64.8 us
  Pallas kernels  63.5 us (98%)
  local copies, waits for them, and re-layouts  1.32 us (2%)
    pallas_call x1, Pallas kernels, per_device(): pl.pallas_call(kernel, name='scan', out_shape=pltpu.VMEM((ROWS, HEADS * W...  63.5 us
    unnamed x1, local copies, waits for them, and re-layouts  1.32 us

profile of v2, /device:TPU:1, one launch (start us, length us, event | category | flops | bytes accessed | tf_op | source)
XLA Modules:
  0.0 64.8 jit_solution(11567301284310215298)
XLA Ops:
  0.0 63.5 %scan.1 = bf16[128,8192]{1,0:T(8,128)(2,1)S(1)} custom-call(bf16[128,8192]{1,0:T(8,128)(2,1)} %x_hbm.1, bf16[1024,128]{1,0:T(8,128)(2,1)} %bitcast.5, bf16[1024,128]{1,0:T(8,128)(2,1)} %bitcast.6, bf16[128,128]{1,0:T(8,128)(2,1)} %dt_hbm.1, f32[1,128]{1,0:T(1,128)} %bitcast.7, f32[1,128]{1,0:T(1,128)} %bitcast.8, f32[1,128]{1,0:T(1,128)} %bitcast.9), custom_call_target="tpu_custom_call" | custom-call | tf_op jit(solution)/shard_map/scan/pallas_call | solution.py:398
  63.5 1.3 %copy.9 = bf16[128,8192]{1,0:T(8,128)(2,1)} copy(bf16[128,8192]{1,0:T(8,128)(2,1)S(1)} %scan.1) | data formatting | bytes 4194304

commit v3 on v2

--- a/solution.py
+++ b/solution.py
@@ -42,7 +42,7 @@
     dt_ref, rate_ref, bias_ref, skip_ref, xv, bv, cv, bg, cg, spread, end_parts, in_parts, skip_parts, cum_cols, cum_rows, dt_rows,
     s_out, s_in, p_out, p_in, acc, ew,
     log_own, log_all, shard_own, shard_all, pair_out, pair_in, zsum_own, zsum_in, back_out, back_in,
-    end_rows, z_rows, total_state, before_state, firsts,
+    end_rows, z_rows, total_state, before_state, firsts, ready,
     load_sem, b_sem, s_send, s_recv, p_send, p_recv, log_send, log_recv,
     shard_send, shard_recv, core_send, core_recv, z_send, z_recv, back_send, back_recv,
 ):
@@ -121,11 +121,11 @@
 
     lax.fori_loop(1, SHARDS, greet_head, 0)
 
-    def greet_z(back, carry):
-        pl.semaphore_signal(barrier, inc=1, device_id=(back * 2 + core, me), device_id_type=MESH)
-        return carry
-
-    lax.fori_loop(0, z, greet_z, 0)
+    def greet_z(to, carry):
+        pl.semaphore_signal(barrier, inc=1, device_id=(to * 2 + core, me), device_id_type=MESH)
+        return carry
+
+    lax.fori_loop(z + 1, ZS, greet_z, 0)
     pl.semaphore_signal(barrier, inc=1, device_id=(other, me), device_id_type=MESH)
 
     for load in small:
@@ -164,7 +164,13 @@
     b_load.wait()
     regroup(bv, bg)
 
-    pl.semaphore_wait(barrier, SHARDS - 1 + ZS - 1 - z + 1)
+    pl.semaphore_wait(barrier, SHARDS - 1 + z + 1)
+
+    def tell_back(back, carry):
+        pl.semaphore_signal(ready, inc=1, device_id=(back * 2 + core, me), device_id_type=MESH)
+        return carry
+
+    lax.fori_loop(0, z, tell_back, 0)
 
     def send_logs(i, carry):
         log_copy(peer(i, 1), me).start()
@@ -253,27 +259,32 @@
     lax.fori_loop(2, 4, inside, 0)
     shard_core_wait().wait_recv()
 
-    def send_shard(to, carry):
-        shard_copy(to, z).start()
-        return carry
-
-    lax.fori_loop(z + 1, ZS, send_shard, 0)
-
-    def shard_wait(src, carry):
-        shard_copy(src, src).wait_recv()
-        return carry
-
-    lax.fori_loop(0, z, shard_wait, 0)
-    shard_all[z] = shard_own[...]
-    shard_logs = shard_all[:, :, 0, :]
-    pair_logs = shard_logs[:, 0, :] + shard_logs[:, 1, :]
-    zi, zj = iota((ZS, ZS), 0), iota((ZS, ZS), 1)
-    between = ((zj > zi) & (zj < z)).astype(F32)
-    z_logs = dot(between, pair_logs, precision=HI)
-    z_weight = jnp.exp(dot(z_logs, mine, precision=HI))
-    for j in range(ZS):
-        z_rows[j] = jnp.broadcast_to(z_weight[j : j + 1, :], (8, OWN))
-    pair_decay = jnp.exp(dot(shard_all[z, :, 0, :], mine, precision=HI))
+    pair_decay = jnp.exp(dot(shard_own[:, 0, :], mine, precision=HI))
+
+    def exchange_logs():
+        @pl.when(z < ZS - 1)
+        def _():
+            pl.semaphore_wait(ready, ZS - 1 - z)
+
+        def send_shard(to, carry):
+            shard_copy(to, z).start()
+            return carry
+
+        lax.fori_loop(z + 1, ZS, send_shard, 0)
+
+    def z_tables():
+        def shard_wait(src, carry):
+            shard_copy(src, src).wait_recv()
+            return carry
+
+        lax.fori_loop(0, z, shard_wait, 0)
+        pair_logs = shard_all[:, 0, 0, :] + shard_all[:, 1, 0, :]
+        zi, zj = iota((ZS, ZS), 0), iota((ZS, ZS), 1)
+        between = ((zj > zi) & (zj < z)).astype(F32)
+        z_logs = dot(between, pair_logs, precision=HI)
+        z_weight = jnp.exp(dot(z_logs, mine, precision=HI))
+        for j in range(ZS):
+            z_rows[j] = jnp.broadcast_to(z_weight[j : j + 1, :], (8, OWN))
 
     def half(value, which):
         return jnp.where(which == 0, value[:HALF, :], value[HALF:, :])
@@ -345,9 +356,11 @@
         value = (acc[k, :, cols] + ew[k, :, cols] * across).astype(BF)
         y_ref[:, pl.ds(pl.multiple_of(k * OWN + p * COLS, COLS), COLS)] = value
 
+    exchange_logs()
     gather(0)
     lax.fori_loop(4, 6, inside, 0)
     gather(1)
+    z_tables()
     give_back(0)
     lax.fori_loop(6, 7, inside, 0)
     gather(2)
@@ -439,6 +452,7 @@
             vmem((STATE, COLS), F32),
             vmem((HALF, COLS), F32),
             vmem((PIECES, HALF, COLS), F32),
+            pltpu.SemaphoreType.REGULAR,
             dma((GROUPS,)),
             dma((6,)),
             dma((PIECES, SHARDS)),

time: 64.9 us -> 60.6 us (0.934)
  Pallas kernels: 63.5 us -> 59.2 us
    pallas_call x1, Pallas kernels: 63.5 us -> 59.2 us  [per_device(): pl.pallas_call(kernel, name='scan', out_shape=pltpu.VMEM((ROWS, HEADS * W...]
where the time goes in v3:
time: 60.6 us; the launch traced here: 60.5 us
  Pallas kernels  59.2 us (98%)
  local copies, waits for them, and re-layouts  1.32 us (2%)
    pallas_call x1, Pallas kernels, per_device(): pl.pallas_call(kernel, name='scan', out_shape=pltpu.VMEM((ROWS, HEADS * W...  59.2 us
    unnamed x1, local copies, waits for them, and re-layouts  1.32 us

profile of v3, /device:TPU:1, one launch (start us, length us, event | category | flops | bytes accessed | tf_op | source)
XLA Modules:
  0.0 60.5 jit_solution(15552986091775659931)
XLA Ops:
  0.0 59.2 %scan.1 = bf16[128,8192]{1,0:T(8,128)(2,1)S(1)} custom-call(bf16[128,8192]{1,0:T(8,128)(2,1)} %x_hbm.1, bf16[1024,128]{1,0:T(8,128)(2,1)} %bitcast.5, bf16[1024,128]{1,0:T(8,128)(2,1)} %bitcast.6, bf16[128,128]{1,0:T(8,128)(2,1)} %dt_hbm.1, f32[1,128]{1,0:T(1,128)} %bitcast.7, f32[1,128]{1,0:T(1,128)} %bitcast.8, f32[1,128]{1,0:T(1,128)} %bitcast.9), custom_call_target="tpu_custom_call" | custom-call | tf_op jit(solution)/shard_map/scan/pallas_call | solution.py:411
  59.2 1.3 %copy.9 = bf16[128,8192]{1,0:T(8,128)(2,1)} copy(bf16[128,8192]{1,0:T(8,128)(2,1)S(1)} %scan.1) | data formatting | bytes 4194304

commit v4 on v3

--- a/solution.py
+++ b/solution.py
@@ -369,25 +369,11 @@
     gather(3)
     give_back(2)
     give_back(3)
-    for p in range(PIECES):
-        finish(p, me)
-
-        def p_wait(i, carry):
-            batch = [peer(3 * i + 1 + j, -1) for j in range(3)]
-            for src in batch:
-                p_copy(p, src, src).wait_recv()
-            for src in batch:
-                finish(p, src)
-            return carry
-
-        lax.fori_loop(0, (SHARDS - 1) // 3, p_wait, 0)
-
     def sent_head(i, carry):
         to = peer(i, 1)
         log_copy(to, me).wait_send()
         for p in range(PIECES):
             s_copy(p, to, me).wait_send()
-            p_copy(p, to, me).wait_send()
         return carry
 
     lax.fori_loop(1, SHARDS, sent_head, 0)
@@ -403,6 +389,27 @@
     for p in range(PIECES):
         pair_copy(p).wait_send()
         back_copy(p).wait_send()
+
+    for p in range(PIECES):
+        if p == PIECES - 1:
+            for q in range(PIECES):
+
+                def sent_p(i, carry):
+                    p_copy(q, peer(i, 1), me).wait_send()
+                    return carry
+
+                lax.fori_loop(1, SHARDS, sent_p, 0)
+        finish(p, me)
+
+        def p_wait(i, carry):
+            batch = [peer(5 * i + 1 + j, -1) for j in range(5)]
+            for src in batch:
+                p_copy(p, src, src).wait_recv()
+            for src in batch:
+                finish(p, src)
+            return carry
+
+        lax.fori_loop(0, (SHARDS - 1) // 5, p_wait, 0)
 
 
 def per_device(x_in, b_in, c_in, dt_raw, decay_rate, dt_bias, skip_gain):

time: 60.6 us -> 60.5 us (level)
  no operation moved by 1% of the time
where the time goes in v4:
time: 60.5 us; the launch traced here: 60 us
  Pallas kernels  58.7 us (97%)
  local copies, waits for them, and re-layouts  1.32 us (2%)
    pallas_call x1, Pallas kernels, per_device(): pl.pallas_call(kernel, name='scan', out_shape=pltpu.VMEM((ROWS, HEADS * W...  58.7 us
    unnamed x1, local copies, waits for them, and re-layouts  1.32 us

profile of v4, /device:TPU:1, one launch (start us, length us, event | category | flops | bytes accessed | tf_op | source)
XLA Modules:
  0.0 60.0 jit_solution(9457521774227388142)
XLA Ops:
  0.0 58.7 %scan.1 = bf16[128,8192]{1,0:T(8,128)(2,1)S(1)} custom-call(bf16[128,8192]{1,0:T(8,128)(2,1)} %x_hbm.1, bf16[1024,128]{1,0:T(8,128)(2,1)} %bitcast.5, bf16[1024,128]{1,0:T(8,128)(2,1)} %bitcast.6, bf16[128,128]{1,0:T(8,128)(2,1)} %dt_hbm.1, f32[1,128]{1,0:T(1,128)} %bitcast.7, f32[1,128]{1,0:T(1,128)} %bitcast.8, f32[1,128]{1,0:T(1,128)} %bitcast.9), custom_call_target="tpu_custom_call" | custom-call | tf_op jit(solution)/shard_map/scan/pallas_call | solution.py:418
  58.7 1.3 %copy.9 = bf16[128,8192]{1,0:T(8,128)(2,1)} copy(bf16[128,8192]{1,0:T(8,128)(2,1)S(1)} %scan.1) | data formatting | bytes 4194304
